TPU v7x, 32 devices: a whole 2x2x4 slice. The times are simulated.
32 devices in a mesh: dp: 8 (over y, x, core), tensor: 4 (over z).
Axes of the slice: x: 2, y: 2, z: 4, core: 2. Of those that a mesh axis runs over, the one named last changes fastest.
Arguments:
- hidden: bfloat16 [4096, 8192], P(('dp', 'tensor')), may hold values from -6 to 6
- norm_gain: float32 [8192], replicated, may hold values from 0.5 to 1.5
- tile_values: bfloat16 [4, 80, 128, 128], P('tensor', 'dp'), may hold values from -0.15625 to 0.15625
- tile_ids: int32 [4, 80], P('tensor', 'dp'), may hold values from 0 to 1279, as said below
- tile_counts: int32 [4, 8], P('tensor', 'dp'), may hold values from 5 to 10, as said below
- proj_grad: bfloat16 [4096, 10240], P('dp', 'tensor'), may hold values from -6 to 6
Outputs:
- projections: bfloat16 [4096, 10240], P('dp', 'tensor')
- hidden_grad: bfloat16 [4096, 8192], P(('dp', 'tensor'))
- tile_grads: float32 [4, 80, 128, 128], P('tensor', 'dp')
- gain_grad: float32 [8192], replicated
Inputs may be any that keep to these rules, and one draw needn't show every extreme that they name: `tile_ids`: within each tensor index the 80 block numbers are distinct; a slot's number holds whether or not the slot is live. `tile_counts`: for every tensor index some owner has all 10 slots live.
All inputs are finite; a program needn't handle non-finite values.
Results may differ from a plain program's by a relative error of at most 0.013.
Values may be sent and summed in bfloat16 or wider, within the bound.
A program may use at most 192 MiB of HBM per device.

v0:
```python
import math
import jax
import jax.numpy as jnp
from jax import lax
from jax.sharding import PartitionSpec as P

EPSILON = 1e-05


def normalize(source, norm_gain):
    source_f = source.astype(jnp.float32)
    inverse = lax.rsqrt(jnp.mean(source_f * source_f, axis=-1, keepdims=True) + EPSILON)
    return (source_f, inverse, (source_f * inverse * norm_gain).astype(jnp.bfloat16))


def selector(block_names, total_count):
    return (block_names[:, None] == jnp.arange(total_count, dtype=jnp.int32)[None, :]).astype(
        jnp.bfloat16
    )


def pick_tiles(blocks, block_names, total_count):
    chooser = selector(block_names, total_count)
    return jnp.einsum("nri,sr->nsi", blocks, chooser, preferred_element_type=jnp.float32).astype(
        jnp.bfloat16
    )


def place_tiles(values, block_names, total_count):
    chooser = selector(block_names, total_count)
    upper_half = values.astype(jnp.bfloat16)
    lower_half = (values - upper_half.astype(jnp.float32)).astype(jnp.bfloat16)
    placed = jnp.einsum("nsi,sr->nri", upper_half, chooser, preferred_element_type=jnp.float32)
    return placed + jnp.einsum(
        "nsi,sr->nri", lower_half, chooser, preferred_element_type=jnp.float32
    )


def over_groups(handler, running, tile_block, tile_names, anchor, slot_count):
    group_total = tile_names.shape[0] // slot_count

    def loop_step(group_idx, state):
        offset = group_idx * slot_count
        block_vals = lax.dynamic_slice_in_dim(tile_block, offset, slot_count, 0)
        block_names = lax.dynamic_slice_in_dim(tile_names, offset, slot_count, 0)
        return handler(state, block_vals, block_names, anchor + offset)

    return lax.fori_loop(0, group_total, loop_step, running)


def body(hidden, norm_gain, tile_values, tile_ids, tile_counts, proj_grad):
    model_width = hidden.shape[1]
    tile_size = tile_values.shape[-1]
    slot_count = tile_values.shape[1]
    seq_rows = proj_grad.shape[0]
    col_tiles = proj_grad.shape[1] // tile_size
    row_tiles = model_width // tile_size
    live_mask = (jnp.arange(slot_count) < tile_counts[0, 0]).astype(jnp.bfloat16)
    masked = tile_values[0] * live_mask[:, None, None]
    own_names = tile_ids[0]
    hidden_f, inverse, normed = normalize(hidden, norm_gain)
    gathered = lax.all_gather(normed, "tensor", axis=0, tiled=True)
    x_blocks = gathered.reshape(seq_rows, row_tiles, tile_size)
    g_blocks = proj_grad.reshape(seq_rows, col_tiles, tile_size)

    def forward_group(running, block_vals, block_names, offset):
        picked = pick_tiles(x_blocks, block_names // col_tiles, row_tiles)
        parts = jnp.einsum("nsi,sij->nsj", picked, block_vals, preferred_element_type=jnp.float32)
        return running + place_tiles(parts, block_names % col_tiles, col_tiles)

    start_out = jnp.zeros((seq_rows, col_tiles, tile_size), jnp.float32)
    all_vals, all_names = (
        lax.all_gather(masked, "dp", axis=0, tiled=True),
        lax.all_gather(own_names, "dp", axis=0, tiled=True),
    )
    outputs = over_groups(forward_group, start_out, all_vals, all_names, 0, slot_count)
    projections = outputs.reshape(seq_rows, col_tiles * tile_size).astype(jnp.bfloat16)
    slot_total_all = all_names.shape[0]

    def row_grad_of(g_part):

        def backward_group(local_grad, block_vals, block_names, offset):
            picked_g = pick_tiles(g_part, block_names % col_tiles, col_tiles)
            backward = jnp.einsum(
                "nsj,sij->nsi", picked_g, block_vals, preferred_element_type=jnp.float32
            )
            return local_grad + place_tiles(backward, block_names // col_tiles, row_tiles)

        start_grad = jnp.zeros((g_part.shape[0], row_tiles, tile_size), jnp.float32)
        local_grad = over_groups(backward_group, start_grad, all_vals, all_names, 0, slot_count)
        return local_grad.reshape(g_part.shape[0], model_width).astype(jnp.bfloat16)

    def tile_grad_of(weight_grad, x_part, g_part):

        def tile_group(tile_acc, block_vals, block_names, offset):
            picked_x = pick_tiles(x_part, block_names // col_tiles, row_tiles)
            picked_g = pick_tiles(g_part, block_names % col_tiles, col_tiles)
            tile_part = jnp.einsum(
                "nsi,nsj->sij", picked_x, picked_g, preferred_element_type=jnp.float32
            )
            current = lax.dynamic_slice_in_dim(tile_acc, offset, tile_part.shape[0], 0)
            return lax.dynamic_update_slice_in_dim(tile_acc, current + tile_part, offset, 0)

        return over_groups(tile_group, weight_grad, all_vals, all_names, 0, slot_count)

    block_rows = math.gcd(seq_rows, 256)
    start_tiles = jnp.zeros((slot_total_all, tile_size, tile_size), jnp.float32)

    def row_block(block_idx, state):
        row_grad, weight_grad = state
        begin = block_idx * block_rows
        x_part = lax.dynamic_slice_in_dim(x_blocks, begin, block_rows, 0)
        g_part = lax.dynamic_slice_in_dim(g_blocks, begin, block_rows, 0)
        rounded = row_grad_of(g_part)
        row_grad = lax.dynamic_update_slice_in_dim(row_grad, rounded, begin, 0)
        weight_grad = tile_grad_of(weight_grad, x_part, g_part)
        return (row_grad, weight_grad)

    initial_back = (jnp.zeros((seq_rows, model_width), jnp.bfloat16), start_tiles)
    row_grad, weight_grad = lax.fori_loop(0, seq_rows // block_rows, row_block, initial_back)
    row_sum = lax.psum_scatter(row_grad, "tensor", scatter_dimension=0, tiled=True).astype(
        jnp.float32
    )
    tile_sum = lax.psum_scatter(
        weight_grad.astype(jnp.bfloat16), "dp", scatter_dimension=0, tiled=True
    ).astype(jnp.float32)
    tile_grads = (tile_sum * live_mask.astype(jnp.float32)[:, None, None])[None]
    unit = hidden_f * inverse
    gain_part = jnp.sum(row_sum * unit, axis=0)
    gain_grad = lax.psum(gain_part, ("dp", "tensor"))
    scaled = row_sum * norm_gain
    hidden_grad = (
        inverse * (scaled - unit * jnp.mean(scaled * unit, axis=-1, keepdims=True))
    ).astype(jnp.bfloat16)
    return (projections, hidden_grad, tile_grads, gain_grad)


def solution(mesh):
    in_specs = (
        P(("dp", "tensor"), None),
        P(),
        P("tensor", "dp", None, None),
        P("tensor", "dp"),
        P("tensor", "dp"),
        P("dp", "tensor"),
    )
    out_specs = (P("dp", "tensor"), P(("dp", "tensor"), None), P("tensor", "dp", None, None), P())
    return jax.shard_map(body, mesh=mesh, in_specs=in_specs, out_specs=out_specs, check_vma=False)
```

profile of v0, /device:TPU:0, one launch (start us, length us, event | category | flops | bytes accessed | tf_op | source)
XLA Modules:
  0.0 951.3 jit_solution(16404277503629230293)
XLA Ops:
  20.3 9.5 all-reduce
  29.8 135.6 %all-gather.6.cloned.1.call-done = bf16[512,8192]{1,0:T(8,128)(2,1)} async-done(((bf16[128,8192]{1,0:T(8,128)(2,1)}), bf16[512,8192]{1,0:T(8,128)(2,1)}) %all-gather.6.cloned.1.call-update) | async-done | bytes 8388624 | tf_op jit(solution)/shard_map/all_gather | solution.py:62
  165.4 9.4 copy.42
  174.7 21.4 %all-gather.4.cloned.1.call-done = bf16[80,128,128]{2,1,0:T(8,128)(2,1)} async-done(((bf16[10,128,128]{2,1,0:T(8,128)(2,1)}), bf16[80,128,128]{2,1,0:T(8,128)(2,1)}) %all-gather.4.cloned.1.call-update) | async-done | bytes 2621456 | tf_op jit(solution)/shard_map/all_gather | solution.py:73
  203.4 463.0 %while.101 = (s32[]{:T(128)}, bf16[512,8192]{1,0:T(8,128)(2,1)}, f32[80,128,128]{2,1,0:T(8,128)}, bf16[512,20,128]{0,2,1:T(8,128)(2,1)}, s32[80]{0:T(128)S(1)}, ...) while((s32[]{:T(128)}, bf16[512,8192]{1,0:T(8,128)(2,1)}, ...), condition=%wide.region_8.9_spmd, body=%wide.region_3.8_spmd.sunk | while | flops 330664448 | bytes 85787744 | solution.py:120
  205.9 162.2 %while.103 = (s32[]{:T(128)}, f32[256,64,128]{2,1,0:T(8,128)}, s32[80]{0:T(128)S(1)}, bf16[80,128,128]{2,1,0:T(8,128)(2,1)}, bf16[256,20,128]{2,1,0:T(8,128)(2,1...) while((s32[]{:T(128)}, f32[256,64,128]{2,1,0:T(8,128)}, s32[80]{0:T(128)S(1)}, ...), condition=%wide.region_5.5_spmd.clone, body=%wide.region_4.4_spmd.clone.sunk | while | flops 188810816 | bytes 41746828 | solution.py:48
  216.1 8.0 bitcast_add_fusion.5
  234.3 10.4 %bitcast_add_fusion.5 = f32[256,64,128]{2,1,0:T(8,128)} fusion(f32[256,64,128]{2,1,0:T(8,128)} %get-tuple-element.990, f32[64,256,128]{2,0,1:T(8,128)} %fusion.97, pred[]{:T(512)S(6)} %compare.7, bf16[256,10,128]{2,1,0:T(8,128)(2,1)S(1)} %copy.73, s32[10]{0:T(128)S(1)} %get-tuple-element.971), kind=kOutput, calls=%fused_computation.16.clone.1 | convolution fusion | flops 48235136 | bytes 25821224 | tf_op jit(solution)/shard_map/while/body/eval_jaxpr/while/body/eval_jaxpr/nsi,sr->nri/dot_general | solution.py:34
  254.8 10.4 %bitcast_add_fusion.5 = f32[256,64,128]{2,1,0:T(8,128)} fusion(f32[256,64,128]{2,1,0:T(8,128)} %get-tuple-element.990, f32[64,256,128]{2,0,1:T(8,128)} %fusion.97, pred[]{:T(512)S(6)} %compare.7, bf16[256,10,128]{2,1,0:T(8,128)(2,1)S(1)} %copy.73, s32[10]{0:T(128)S(1)} %get-tuple-element.971), kind=kOutput, calls=%fused_computation.16.clone.1 | convolution fusion | flops 48235136 | bytes 25821224 | tf_op jit(solution)/shard_map/while/body/eval_jaxpr/while/body/eval_jaxpr/nsi,sr->nri/dot_general | solution.py:34
  275.4 10.4 %bitcast_add_fusion.5 = f32[256,64,128]{2,1,0:T(8,128)} fusion(f32[256,64,128]{2,1,0:T(8,128)} %get-tuple-element.990, f32[64,256,128]{2,0,1:T(8,128)} %fusion.97, pred[]{:T(512)S(6)} %compare.7, bf16[256,10,128]{2,1,0:T(8,128)(2,1)S(1)} %copy.73, s32[10]{0:T(128)S(1)} %get-tuple-element.971), kind=kOutput, calls=%fused_computation.16.clone.1 | convolution fusion | flops 48235136 | bytes 25821224 | tf_op jit(solution)/shard_map/while/body/eval_jaxpr/while/body/eval_jaxpr/nsi,sr->nri/dot_general | solution.py:34
  296.0 10.4 %bitcast_add_fusion.5 = f32[256,64,128]{2,1,0:T(8,128)} fusion(f32[256,64,128]{2,1,0:T(8,128)} %get-tuple-element.990, f32[64,256,128]{2,0,1:T(8,128)} %fusion.97, pred[]{:T(512)S(6)} %compare.7, bf16[256,10,128]{2,1,0:T(8,128)(2,1)S(1)} %copy.73, s32[10]{0:T(128)S(1)} %get-tuple-element.971), kind=kOutput, calls=%fused_computation.16.clone.1 | convolution fusion | flops 48235136 | bytes 25821224 | tf_op jit(solution)/shard_map/while/body/eval_jaxpr/while/body/eval_jaxpr/nsi,sr->nri/dot_general | solution.py:34
  316.5 10.4 %bitcast_add_fusion.5 = f32[256,64,128]{2,1,0:T(8,128)} fusion(f32[256,64,128]{2,1,0:T(8,128)} %get-tuple-element.990, f32[64,256,128]{2,0,1:T(8,128)} %fusion.97, pred[]{:T(512)S(6)} %compare.7, bf16[256,10,128]{2,1,0:T(8,128)(2,1)S(1)} %copy.73, s32[10]{0:T(128)S(1)} %get-tuple-element.971), kind=kOutput, calls=%fused_computation.16.clone.1 | convolution fusion | flops 48235136 | bytes 25821224 | tf_op jit(solution)/shard_map/while/body/eval_jaxpr/while/body/eval_jaxpr/nsi,sr->nri/dot_general | solution.py:34
  337.1 10.4 %bitcast_add_fusion.5 = f32[256,64,128]{2,1,0:T(8,128)} fusion(f32[256,64,128]{2,1,0:T(8,128)} %get-tuple-element.990, f32[64,256,128]{2,0,1:T(8,128)} %fusion.97, pred[]{:T(512)S(6)} %compare.7, bf16[256,10,128]{2,1,0:T(8,128)(2,1)S(1)} %copy.73, s32[10]{0:T(128)S(1)} %get-tuple-element.971), kind=kOutput, calls=%fused_computation.16.clone.1 | convolution fusion | flops 48235136 | bytes 25821224 | tf_op jit(solution)/shard_map/while/body/eval_jaxpr/while/body/eval_jaxpr/nsi,sr->nri/dot_general | solution.py:34
  357.7 10.4 %bitcast_add_fusion.5 = f32[256,64,128]{2,1,0:T(8,128)} fusion(f32[256,64,128]{2,1,0:T(8,128)} %get-tuple-element.990, f32[64,256,128]{2,0,1:T(8,128)} %fusion.97, pred[]{:T(512)S(6)} %compare.7, bf16[256,10,128]{2,1,0:T(8,128)(2,1)S(1)} %copy.73, s32[10]{0:T(128)S(1)} %get-tuple-element.971), kind=kOutput, calls=%fused_computation.16.clone.1 | convolution fusion | flops 48235136 | bytes 25821224 | tf_op jit(solution)/shard_map/while/body/eval_jaxpr/while/body/eval_jaxpr/nsi,sr->nri/dot_general | solution.py:34
  372.5 10.0 %bitcast_dynamic-update-slice_fusion.3 = bf16[512,8192]{1,0:T(8,128)(2,1)} fusion(bf16[512,8192]{1,0:T(8,128)(2,1)} %get-tuple-element.1081, s32[]{:T(128)S(6)} %select_n.148, bf16[32,8,64,128]{3,2,1,0:T(8,128)(2,1)S(1)} %bitcast.116), kind=kLoop, calls=%fused_computation.34.clone.1 | loop fusion | bytes 8388612 | tf_op jit(solution)/shard_map/while/body/eval_jaxpr/dynamic_update_slice | solution.py:115
  382.6 5.2 constant_dynamic-slice_fusion.5
  387.7 47.1 %while.104 = (s32[]{:T(128)}, f32[80,128,128]{2,1,0:T(8,128)}, s32[80]{0:T(128)S(1)}, bf16[256,64,128]{2,1,0:T(8,128)(2,1)}, bf16[256,20,128]{2,1,0:T(8,128)(2,1...) while((s32[]{:T(128)}, f32[80,128,128]{2,1,0:T(8,128)}, s32[80]{0:T(128)S(1)}, ...), condition=%wide.region_7.7_spmd, body=%wide.region_6.6_spmd.sunk | while | flops 139756480 | bytes 9437531 | solution.py:48
  437.4 162.2 %while.103 = (s32[]{:T(128)}, f32[256,64,128]{2,1,0:T(8,128)}, s32[80]{0:T(128)S(1)}, bf16[80,128,128]{2,1,0:T(8,128)(2,1)}, bf16[256,20,128]{2,1,0:T(8,128)(2,1...) while((s32[]{:T(128)}, f32[256,64,128]{2,1,0:T(8,128)}, s32[80]{0:T(128)S(1)}, ...), condition=%wide.region_5.5_spmd.clone, body=%wide.region_4.4_spmd.clone.sunk | while | flops 188810816 | bytes 41746828 | solution.py:48
  447.6 8.0 bitcast_add_fusion.5
  465.7 10.4 %bitcast_add_fusion.5 = f32[256,64,128]{2,1,0:T(8,128)} fusion(f32[256,64,128]{2,1,0:T(8,128)} %get-tuple-element.990, f32[64,256,128]{2,0,1:T(8,128)} %fusion.97, pred[]{:T(512)S(6)} %compare.7, bf16[256,10,128]{2,1,0:T(8,128)(2,1)S(1)} %copy.73, s32[10]{0:T(128)S(1)} %get-tuple-element.971), kind=kOutput, calls=%fused_computation.16.clone.1 | convolution fusion | flops 48235136 | bytes 25821224 | tf_op jit(solution)/shard_map/while/body/eval_jaxpr/while/body/eval_jaxpr/nsi,sr->nri/dot_general | solution.py:34
  486.3 10.4 %bitcast_add_fusion.5 = f32[256,64,128]{2,1,0:T(8,128)} fusion(f32[256,64,128]{2,1,0:T(8,128)} %get-tuple-element.990, f32[64,256,128]{2,0,1:T(8,128)} %fusion.97, pred[]{:T(512)S(6)} %compare.7, bf16[256,10,128]{2,1,0:T(8,128)(2,1)S(1)} %copy.73, s32[10]{0:T(128)S(1)} %get-tuple-element.971), kind=kOutput, calls=%fused_computation.16.clone.1 | convolution fusion | flops 48235136 | bytes 25821224 | tf_op jit(solution)/shard_map/while/body/eval_jaxpr/while/body/eval_jaxpr/nsi,sr->nri/dot_general | solution.py:34
  506.9 10.4 %bitcast_add_fusion.5 = f32[256,64,128]{2,1,0:T(8,128)} fusion(f32[256,64,128]{2,1,0:T(8,128)} %get-tuple-element.990, f32[64,256,128]{2,0,1:T(8,128)} %fusion.97, pred[]{:T(512)S(6)} %compare.7, bf16[256,10,128]{2,1,0:T(8,128)(2,1)S(1)} %copy.73, s32[10]{0:T(128)S(1)} %get-tuple-element.971), kind=kOutput, calls=%fused_computation.16.clone.1 | convolution fusion | flops 48235136 | bytes 25821224 | tf_op jit(solution)/shard_map/while/body/eval_jaxpr/while/body/eval_jaxpr/nsi,sr->nri/dot_general | solution.py:34
  527.4 10.4 %bitcast_add_fusion.5 = f32[256,64,128]{2,1,0:T(8,128)} fusion(f32[256,64,128]{2,1,0:T(8,128)} %get-tuple-element.990, f32[64,256,128]{2,0,1:T(8,128)} %fusion.97, pred[]{:T(512)S(6)} %compare.7, bf16[256,10,128]{2,1,0:T(8,128)(2,1)S(1)} %copy.73, s32[10]{0:T(128)S(1)} %get-tuple-element.971), kind=kOutput, calls=%fused_computation.16.clone.1 | convolution fusion | flops 48235136 | bytes 25821224 | tf_op jit(solution)/shard_map/while/body/eval_jaxpr/while/body/eval_jaxpr/nsi,sr->nri/dot_general | solution.py:34
  548.0 10.4 %bitcast_add_fusion.5 = f32[256,64,128]{2,1,0:T(8,128)} fusion(f32[256,64,128]{2,1,0:T(8,128)} %get-tuple-element.990, f32[64,256,128]{2,0,1:T(8,128)} %fusion.97, pred[]{:T(512)S(6)} %compare.7, bf16[256,10,128]{2,1,0:T(8,128)(2,1)S(1)} %copy.73, s32[10]{0:T(128)S(1)} %get-tuple-element.971), kind=kOutput, calls=%fused_computation.16.clone.1 | convolution fusion | flops 48235136 | bytes 25821224 | tf_op jit(solution)/shard_map/while/body/eval_jaxpr/while/body/eval_jaxpr/nsi,sr->nri/dot_general | solution.py:34
  568.6 10.4 %bitcast_add_fusion.5 = f32[256,64,128]{2,1,0:T(8,128)} fusion(f32[256,64,128]{2,1,0:T(8,128)} %get-tuple-element.990, f32[64,256,128]{2,0,1:T(8,128)} %fusion.97, pred[]{:T(512)S(6)} %compare.7, bf16[256,10,128]{2,1,0:T(8,128)(2,1)S(1)} %copy.73, s32[10]{0:T(128)S(1)} %get-tuple-element.971), kind=kOutput, calls=%fused_computation.16.clone.1 | convolution fusion | flops 48235136 | bytes 25821224 | tf_op jit(solution)/shard_map/while/body/eval_jaxpr/while/body/eval_jaxpr/nsi,sr->nri/dot_general | solution.py:34
  589.1 10.4 %bitcast_add_fusion.5 = f32[256,64,128]{2,1,0:T(8,128)} fusion(f32[256,64,128]{2,1,0:T(8,128)} %get-tuple-element.990, f32[64,256,128]{2,0,1:T(8,128)} %fusion.97, pred[]{:T(512)S(6)} %compare.7, bf16[256,10,128]{2,1,0:T(8,128)(2,1)S(1)} %copy.73, s32[10]{0:T(128)S(1)} %get-tuple-element.971), kind=kOutput, calls=%fused_computation.16.clone.1 | convolution fusion | flops 48235136 | bytes 25821224 | tf_op jit(solution)/shard_map/while/body/eval_jaxpr/while/body/eval_jaxpr/nsi,sr->nri/dot_general | solution.py:34
  604.0 10.1 %bitcast_dynamic-update-slice_fusion.3 = bf16[512,8192]{1,0:T(8,128)(2,1)} fusion(bf16[512,8192]{1,0:T(8,128)(2,1)} %get-tuple-element.1081, s32[]{:T(128)S(6)} %select_n.148, bf16[32,8,64,128]{3,2,1,0:T(8,128)(2,1)S(1)} %bitcast.116), kind=kLoop, calls=%fused_computation.34.clone.1 | loop fusion | bytes 8388612 | tf_op jit(solution)/shard_map/while/body/eval_jaxpr/dynamic_update_slice | solution.py:115
  614.1 5.2 constant_dynamic-slice_fusion.5
  619.2 47.1 %while.104 = (s32[]{:T(128)}, f32[80,128,128]{2,1,0:T(8,128)}, s32[80]{0:T(128)S(1)}, bf16[256,64,128]{2,1,0:T(8,128)(2,1)}, bf16[256,20,128]{2,1,0:T(8,128)(2,1...) while((s32[]{:T(128)}, f32[80,128,128]{2,1,0:T(8,128)}, s32[80]{0:T(128)S(1)}, ...), condition=%wide.region_7.7_spmd, body=%wide.region_6.6_spmd.sunk | while | flops 139756480 | bytes 9437531 | solution.py:48
  671.5 213.0 %while.102 = (s32[]{:T(128)}, f32[512,20,128]{2,1,0:T(8,128)}, s32[80]{0:T(128)S(1)}, bf16[80,128,128]{2,1,0:T(8,128)(2,1)}, bf16[512,64,128]{2,1,0:T(8,128)(2,1...) while((s32[]{:T(128)}, f32[512,20,128]{2,1,0:T(8,128)}, s32[80]{0:T(128)S(1)}, ...), condition=%wide.region_2.3_spmd.clone, body=%wide.region_1.2_spmd.clone.sunk | while | flops 311297152 | bytes 42795404 | solution.py:48
  681.1 5.4 fusion.89
  689.4 7.4 bitcast_add_fusion.4
  706.5 5.3 fusion.89
  714.7 9.2 bitcast_add_fusion.4
  733.5 5.3 fusion.89
  741.7 9.0 bitcast_add_fusion.4
  760.3 5.3 fusion.89
  768.5 9.0 bitcast_add_fusion.4
  787.0 5.4 fusion.89
  795.3 9.0 bitcast_add_fusion.4
  813.9 5.3 fusion.89
  822.2 9.0 bitcast_add_fusion.4
  840.7 5.3 fusion.89
  848.9 9.0 bitcast_add_fusion.4
  867.4 5.3 fusion.89
  875.6 8.9 bitcast_add_fusion.4
  884.6 5.3 copy.35
  899.9 40.2 %psum.7 = f32[8192]{0:T(1024)} all-reduce(f32[8192]{0:T(1024)S(1)} %get-tuple-element.743), channel_id=1, replica_groups=mesh['dp'=8,'tensor'=4] {'dp','tensor'}, use_global_device_ids=true, to_apply=%region_13.14 | all-reduce | flops 8192 | bytes 65536 | tf_op jit(solution)/shard_map/psum | solution.py:130
  (249 shorter events, 409.1 us)
Async XLA Ops:
  7.2 6.4 copy-start
  7.2 158.2 %all-gather.6.cloned.1.call-start = ((), (), s32[]{:S(2)}) async-start(), calls=%async_computation.3 | async-start | bytes 10485760 | tf_op jit(solution)/shard_map/all_gather | solution.py:62
  9.3 9.5 %copy-start.2 = (f32[128]{0:T(128)}, f32[128]{0:T(128)S(1)}, u32[]{:S(2)}) copy-start(f32[128]{0:T(128)S(1)} %add_rsqrt_fusion) | copy-start | bytes 1540
  12.8 6.0 copy-start.5
  12.9 7.4 copy-start.4
  12.9 183.3 %all-gather.4.cloned.1.call-start = ((), (), s32[]{:S(2)}) async-start(), calls=%async_computation.2 | async-start | bytes 2949120 | tf_op jit(solution)/shard_map/all_gather | solution.py:73
  14.4 879.8 %reduce-scatter.5.cloned.1.call-start = ((), (), s32[]{:S(2)}) async-start(), calls=%async_computation.5 | async-start | bytes 2949120 | tf_op jit(solution)/shard_map/reduce_scatter | solution.py:124
  670.9 225.2 %reduce-scatter.3.cloned.1.call-start = ((), (), s32[]{:S(2)}) async-start(), calls=%async_computation.4 | async-start | bytes 10485760 | tf_op jit(solution)/shard_map/reduce_scatter | solution.py:121
  889.8 6.3 copy-start.1
  889.8 6.3 copy-start.3
Sparse Core Ops, SparseCore 0:
  13.0 152.3 all-gather.5
  167.8 28.3 all-gather.3
  671.1 43.6 reduce-scatter.4
  717.0 144.4 reduce-scatter.2
where the time goes:
time: 955 us; the launch traced here: 951 us
  matrix products  535 us (56%)
  local copies, waits for them, and re-layouts  159 us (17%)
  waiting for transfers between devices  158 us (17%)
  blocking collectives  49.7 us (5%)
  other arithmetic  33.7 us (4%)
  between operations  15.2 us (2%)
    dot_general x24, matrix products, place_tiles(): jnp.einsum('nsi,sr->nri', lower_half, chooser, preferred_element_type=jnp...  232 us
    all_gather x1, waiting for transfers between devices, body(): gathered = lax.all_gather(normed, 'tensor', axis=0, tiled=True)  136 us
    dot_general x24, matrix products, place_tiles(): jnp.einsum('nsi,sr->nri', upper_half, chooser, preferred_element_type=jnp...  115 us
    dot_general x56, matrix products, pick_tiles(): jnp.einsum('nri,sr->nsi', blocks, chooser, preferred_element_type=jnp.flo...  99.9 us
    convert_element_type x24, local copies, waits for them, and re-layouts, place_tiles(): upper_half = values.astype(jnp.bfloat16)  53.1 us
    psum x1, blocking collectives, body(): gain_grad = lax.psum(gain_part, ('dp', 'tensor'))  40.2 us
    convert_element_type x24, local copies, waits for them, and re-layouts, place_tiles(): lower_half = (values - upper_half.astype(jnp.float32)).astype(jnp.bfloat16)  39.5 us
    dot_general x16, matrix products, tile_group(): jnp.einsum('nsi,nsj->sij', picked_x, picked_g, preferred_element_type=jnp...  38.1 us
  transfers between devices with their start and end apart: 4, of which 2 were waited for; matrix products, arithmetic and copies ran while one was open for 25% of the time, Pallas kernels for 0%

commit v1 on v0

--- a/solution.py
+++ b/solution.py
@@ -5,6 +5,25 @@
 from jax.sharding import PartitionSpec as P
 
 EPSILON = 1e-05
+
+
+def ring_gather(value, axis, dim):
+    size, index, rows = (lax.axis_size(axis), lax.axis_index(axis), value.shape[dim])
+    forward = [(i, (i + 1) % size) for i in range(size)]
+    downward = [(i, (i - 1) % size) for i in range(size)]
+    out = jnp.zeros((*value.shape[:dim], size * rows, *value.shape[dim + 1 :]), value.dtype)
+    out = lax.dynamic_update_slice_in_dim(out, value, index * rows, axis=dim)
+    from_left = from_right = value
+    half = size // 2
+    for hop in range(1, half + 1):
+        from_left = lax.ppermute(from_left, axis, forward)
+        out = lax.dynamic_update_slice_in_dim(out, from_left, (index - hop) % size * rows, axis=dim)
+        if hop < size - half:
+            from_right = lax.ppermute(from_right, axis, downward)
+            out = lax.dynamic_update_slice_in_dim(
+                out, from_right, (index + hop) % size * rows, axis=dim
+            )
+    return out
 
 
 def normalize(source, norm_gain):
@@ -70,7 +89,7 @@
 
     start_out = jnp.zeros((seq_rows, col_tiles, tile_size), jnp.float32)
     all_vals, all_names = (
-        lax.all_gather(masked, "dp", axis=0, tiled=True),
+        ring_gather(masked, "dp", 0),
         lax.all_gather(own_names, "dp", axis=0, tiled=True),
     )
     outputs = over_groups(forward_group, start_out, all_vals, all_names, 0, slot_count)

time: 955 us -> 849 us (0.89)
  matrix products: 535 us -> 403 us
  local copies, waits for them, and re-layouts: 159 us -> 204 us
  waiting for transfers between devices: 158 us -> 128 us
    dot_general x24, matrix products: 232 us -> 147 us  [place_tiles(): jnp.einsum('nsi,sr->nri', lower_half, chooser, preferred_element_type=jnp...]
    dot_general x24, matrix products: 115 us -> 64.1 us  [place_tiles(): jnp.einsum('nsi,sr->nri', upper_half, chooser, preferred_element_type=jnp...]
    all_gather x1, waiting for transfers between devices: 136 us -> 104 us  [body(): gathered = lax.all_gather(normed, 'tensor', axis=0, tiled=True)]
    while x0 -> x65, local copies, waits for them, and re-layouts: none -> 30.5 us
    all_gather x1 -> x0, waiting for transfers between devices: 21.4 us -> none  [body(): lax.all_gather(masked, 'dp', axis=0, tiled=True)]
    ppermute x0 -> x7, waiting for transfers between devices: none -> 17.1 us  [the longest x4 15.7 us: ring_gather(): from_left = lax.ppermute(from_left, axis, forward)]
    dot_general x56, matrix products: 99.9 us -> 116 us  [pick_tiles(): jnp.einsum('nri,sr->nsi', blocks, chooser, preferred_element_type=jnp.flo...]
    dot_general x16, matrix products: 34.7 us -> 21.2 us  [backward_group(): jnp.einsum('nsj,sij->nsi', picked_g, block_vals, preferred_element_type=j...]
  transfers between devices with their start and end apart: 4 -> 10, of which waited for: 2 -> 6; matrix products, arithmetic and copies ran while one was open for 25% -> 20% of each run, Pallas kernels for 0% -> 0%
where the time goes in v1:
time: 849 us; the launch traced here: 844 us
  matrix products  403 us (47%)
  local copies, waits for them, and re-layouts  204 us (24%)
  waiting for transfers between devices  128 us (15%)
  blocking collectives  51.2 us (6%)
  other arithmetic  31.7 us (4%)
  between operations  15.3 us (2%)
  starting transfers between devices  9.34 us (1%)
    dot_general x24, matrix products, place_tiles(): jnp.einsum('nsi,sr->nri', lower_half, chooser, preferred_element_type=jnp...  147 us
    dot_general x56, matrix products, pick_tiles(): jnp.einsum('nri,sr->nsi', blocks, chooser, preferred_element_type=jnp.flo...  116 us
    all_gather x1, waiting for transfers between devices, body(): gathered = lax.all_gather(normed, 'tensor', axis=0, tiled=True)  104 us
    dot_general x24, matrix products, place_tiles(): jnp.einsum('nsi,sr->nri', upper_half, chooser, preferred_element_type=jnp...  64.1 us
    convert_element_type x24, local copies, waits for them, and re-layouts, place_tiles(): upper_half = values.astype(jnp.bfloat16)  51 us
    dot_general x16, matrix products, tile_group(): jnp.einsum('nsi,nsj->sij', picked_x, picked_g, preferred_element_type=jnp...  41.9 us
    psum x1, blocking collectives, body(): gain_grad = lax.psum(gain_part, ('dp', 'tensor'))  41.7 us
    convert_element_type x24, local copies, waits for them, and re-layouts, place_tiles(): lower_half = (values - upper_half.astype(jnp.float32)).astype(jnp.bfloat16)  39.5 us
  transfers between devices with their start and end apart: 10, of which 6 were waited for; matrix products, arithmetic and copies ran while one was open for 20% of the time, Pallas kernels for 0%

profile of v1, /device:TPU:0, one launch (start us, length us, event | category | flops | bytes accessed | tf_op | source)
XLA Modules:
  0.0 844.4 jit_solution(4442702809303222131)
XLA Ops:
  18.7 5.6 collective-permute-done
  28.8 4.4 copy.22
  33.3 9.5 %all-reduce = s32[80]{0:T(128)S(1)} all-reduce(s32[80]{0:T(128)S(1)} %bitcast_dynamic-update-slice_fusion.1), channel_id=2, replica_groups=mesh['dp'=8,'tensor'=4] {'dp'}, use_global_device_ids=true, to_apply=%add | all-reduce | flops 80 | bytes 640 | tf_op jit(solution)/shard_map/all_gather | solution.py:93
  53.3 5.9 collective-permute-done.6
  62.2 103.7 %all-gather.3.cloned.1.call-done = bf16[512,8192]{1,0:T(8,128)(2,1)} async-done(((bf16[128,8192]{1,0:T(8,128)(2,1)}), bf16[512,8192]{1,0:T(8,128)(2,1)}) %all-gather.3.cloned.1.call-update) | async-done | bytes 8388624 | tf_op jit(solution)/shard_map/all_gather | solution.py:81
  165.9 9.3 %copy.32 = bf16[64,8,64,128]{3,2,1,0:T(8,128)(2,1)} copy(bf16[64,8,64,128]{3,1,2,0:T(8,128)(2,1)} %bitcast.130) | data formatting | bytes 16777216
  178.3 4.2 broadcast_in_dim.59
  182.6 413.1 %while.101 = (s32[]{:T(128)}, bf16[512,8192]{1,0:T(8,128)(2,1)}, f32[80,128,128]{2,1,0:T(8,128)}, bf16[512,20,128]{0,2,1:T(8,128)(2,1)}, s32[80]{0:T(128)S(1)}, ...) while((s32[]{:T(128)}, bf16[512,8192]{1,0:T(8,128)(2,1)}, ...), condition=%wide.region_8.9_spmd, body=%wide.region_3.8_spmd.sunk | while | flops 329681408 | bytes 87491696 | solution.py:139
  185.1 5.1 constant_dynamic-slice_fusion.5
  190.2 63.1 %while.104 = (s32[]{:T(128)}, f32[80,128,128]{2,1,0:T(8,128)}, s32[80]{0:T(128)S(1)}, bf16[256,64,128]{2,1,0:T(8,128)(2,1)}, bf16[256,20,128]{2,1,0:T(8,128)(2,1...) while((s32[]{:T(128)}, f32[80,128,128]{2,1,0:T(8,128)}, s32[80]{0:T(128)S(1)}, ...), condition=%wide.region_7.7_spmd, body=%wide.region_6.6_spmd.sunk | while | flops 139101120 | bytes 11141467 | solution.py:67
  253.3 121.3 %while.103 = (s32[]{:T(128)}, f32[256,64,128]{2,1,0:T(8,128)}, s32[80]{0:T(128)S(1)}, bf16[80,128,128]{2,1,0:T(8,128)(2,1)}, bf16[256,20,128]{2,1,0:T(8,128)(2,1...) while((s32[]{:T(128)}, f32[256,64,128]{2,1,0:T(8,128)}, s32[80]{0:T(128)S(1)}, ...), condition=%wide.region_5.5_spmd.clone, body=%wide.region_4.4_spmd.clone.sunk | while | flops 188483136 | bytes 41746836 | solution.py:67
  260.5 5.0 bitcast_add_fusion.5
  272.8 8.3 bitcast_add_fusion.5
  288.3 8.3 bitcast_add_fusion.5
  303.9 8.3 bitcast_add_fusion.5
  319.5 8.3 bitcast_add_fusion.5
  335.1 8.3 bitcast_add_fusion.5
  350.7 8.3 bitcast_add_fusion.5
  366.2 8.3 bitcast_add_fusion.5
  374.6 4.5 convert_element_type.269
  379.1 10.0 %bitcast_dynamic-update-slice_fusion.3 = bf16[512,8192]{1,0:T(8,128)(2,1)} fusion(bf16[512,8192]{1,0:T(8,128)(2,1)} %get-tuple-element.1067, s32[]{:T(128)S(6)} %select_n.217, bf16[32,8,64,128]{3,2,1,0:T(8,128)(2,1)S(1)} %bitcast.125), kind=kLoop, calls=%fused_computation.34.clone.1 | loop fusion | bytes 8388612 | tf_op jit(solution)/shard_map/while/body/eval_jaxpr/dynamic_update_slice | solution.py:134
  391.6 5.1 constant_dynamic-slice_fusion.5
  396.7 63.1 %while.104 = (s32[]{:T(128)}, f32[80,128,128]{2,1,0:T(8,128)}, s32[80]{0:T(128)S(1)}, bf16[256,64,128]{2,1,0:T(8,128)(2,1)}, bf16[256,20,128]{2,1,0:T(8,128)(2,1...) while((s32[]{:T(128)}, f32[80,128,128]{2,1,0:T(8,128)}, s32[80]{0:T(128)S(1)}, ...), condition=%wide.region_7.7_spmd, body=%wide.region_6.6_spmd.sunk | while | flops 139101120 | bytes 11141467 | solution.py:67
  459.8 121.3 %while.103 = (s32[]{:T(128)}, f32[256,64,128]{2,1,0:T(8,128)}, s32[80]{0:T(128)S(1)}, bf16[80,128,128]{2,1,0:T(8,128)(2,1)}, bf16[256,20,128]{2,1,0:T(8,128)(2,1...) while((s32[]{:T(128)}, f32[256,64,128]{2,1,0:T(8,128)}, s32[80]{0:T(128)S(1)}, ...), condition=%wide.region_5.5_spmd.clone, body=%wide.region_4.4_spmd.clone.sunk | while | flops 188483136 | bytes 41746836 | solution.py:67
  467.1 5.0 bitcast_add_fusion.5
  479.3 8.3 bitcast_add_fusion.5
  494.9 8.3 bitcast_add_fusion.5
  510.4 8.3 bitcast_add_fusion.5
  526.0 8.3 bitcast_add_fusion.5
  541.6 8.3 bitcast_add_fusion.5
  557.2 8.3 bitcast_add_fusion.5
  572.8 8.3 bitcast_add_fusion.5
  581.1 4.5 convert_element_type.269
  585.6 10.1 %bitcast_dynamic-update-slice_fusion.3 = bf16[512,8192]{1,0:T(8,128)(2,1)} fusion(bf16[512,8192]{1,0:T(8,128)(2,1)} %get-tuple-element.1067, s32[]{:T(128)S(6)} %select_n.217, bf16[32,8,64,128]{3,2,1,0:T(8,128)(2,1)S(1)} %bitcast.125), kind=kLoop, calls=%fused_computation.34.clone.1 | loop fusion | bytes 8388612 | tf_op jit(solution)/shard_map/while/body/eval_jaxpr/dynamic_update_slice | solution.py:134
  595.7 4.5 convert_element_type.186
  600.9 170.0 %while.102 = (s32[]{:T(128)}, f32[512,20,128]{2,1,0:T(8,128)}, s32[80]{0:T(128)S(1)}, bf16[80,128,128]{1,2,0:T(8,128)(2,1)}, bf16[512,64,128]{2,1,0:T(8,128)(2,1...) while((s32[]{:T(128)}, f32[512,20,128]{2,1,0:T(8,128)}, s32[80]{0:T(128)S(1)}, ...), condition=%wide.region_2.3_spmd.clone, body=%wide.region_1.2_spmd.clone.sunk | while | flops 310641792 | bytes 87884280 | solution.py:67
  601.0 4.8 fusion.94
  622.3 4.7 fusion.94
  643.7 4.6 fusion.94
  664.8 4.7 fusion.94
  686.0 4.6 fusion.94
  707.2 4.7 fusion.94
  728.7 4.6 fusion.94
  749.8 4.6 fusion.94
  770.9 5.2 copy.21
  776.1 4.5 copy.25
  782.6 6.5 reduce-scatter.3.cloned.1.call-done
  792.2 41.7 %psum.7 = f32[8192]{0:T(1024)} all-reduce(f32[8192]{0:T(1024)S(1)} %get-tuple-element.727), channel_id=1, replica_groups=mesh['dp'=8,'tensor'=4] {'dp','tensor'}, use_global_device_ids=true, to_apply=%region_13.14 | all-reduce | flops 8192 | bytes 65536 | tf_op jit(solution)/shard_map/psum | solution.py:149
  (362 shorter events, 419.2 us)
Async XLA Ops:
  7.2 7.0 copy-start.4
  7.2 158.8 %all-gather.3.cloned.1.call-start = ((), (), s32[]{:S(2)}) async-start(), calls=%async_computation.2 | async-start | bytes 10485760 | tf_op jit(solution)/shard_map/all_gather | solution.py:81
  13.4 11.4 %copy-start.9 = (u32[32]{0:T(128)S(1)}, u32[32]{0:T(128)}, u32[]{:S(2)}) copy-start(u32[32]{0:T(128)} %constant.336) | copy-start | bytes 388
  13.4 15.3 %copy-start.8 = (s32[1,10]{1,0:T(1,128)S(1)}, s32[1,10]{1,0:T(1,128)}, u32[]{:S(2)}) copy-start(s32[1,10]{1,0:T(1,128)} %param.17) | copy-start | bytes 124
  13.4 767.2 %reduce-scatter.5.cloned.1.call-start = ((), (), s32[]{:S(2)}) async-start(), calls=%async_computation.4 | async-start | bytes 2949120 | tf_op jit(solution)/shard_map/reduce_scatter | solution.py:143
  15.3 9.1 %collective-permute-start = (bf16[10,128,128]{1,2,0:T(8,128)(2,1)S(1)}, bf16[10,128,128]{1,2,0:T(8,128)(2,1)}, u32[]{:S(2)}, u32[]{:S(2)}) collective-permute-start(bf16[10,128,128]{1,2,0:T(8,128)(2,1)S(1)} %get-tuple-element.778), channel_id=1, source_target_pairs={{0,4},{4,8},{8,12},{12,16},{16,20},{20,24},{24,28},{28,0},{1,5},{5... | collective-permute-start | bytes 983048 | tf_op jit(solution)/shard_map/ppermute | solution.py:19
  15.8 10.3 %collective-permute-start.1 = (bf16[10,128,128]{1,2,0:T(8,128)(2,1)S(1)}, bf16[10,128,128]{1,2,0:T(8,128)(2,1)}, u32[]{:S(2)}, u32[]{:S(2)}) collective-permute-start(bf16[10,128,128]{1,2,0:T(8,128)(2,1)S(1)} %get-tuple-element.778), channel_id=1, source_target_pairs={{0,28},{4,0},{8,4},{12,8},{16,12},{20,16},{24,20},{28,24},{1,29},{... | collective-permute-start | bytes 983048 | tf_op jit(solution)/shard_map/ppermute | solution.py:22
  24.4 18.5 %collective-permute-start.2 = (bf16[10,128,128]{1,2,0:T(8,128)(2,1)}, bf16[10,128,128]{1,2,0:T(8,128)(2,1)S(1)}, u32[]{:S(2)}, u32[]{:S(2)}) collective-permute-start(bf16[10,128,128]{1,2,0:T(8,128)(2,1)} %collective-permute-done), channel_id=1, source_target_pairs={{0,4},{4,8},{8,12},{12,16},{16,20},{20,24},{24,28},{28,0},{1,5},{5... | collective-permute-start | bytes 983048 | tf_op jit(solution)/shard_map/ppermute | solution.py:19
  26.1 18.8 %collective-permute-start.3 = (bf16[10,128,128]{1,2,0:T(8,128)(2,1)}, bf16[10,128,128]{1,2,0:T(8,128)(2,1)S(1)}, u32[]{:S(2)}, u32[]{:S(2)}) collective-permute-start(bf16[10,128,128]{1,2,0:T(8,128)(2,1)} %collective-permute-done.1), channel_id=1, source_target_pairs={{0,28},{4,0},{8,4},{12,8},{16,12},{20,16},{24,20},{28,24},{1,29},{... | collective-permute-start | bytes 983048 | tf_op jit(solution)/shard_map/ppermute | solution.py:22
  42.8 9.0 %collective-permute-start.4 = (bf16[10,128,128]{1,2,0:T(8,128)(2,1)S(1)}, bf16[10,128,128]{1,2,0:T(8,128)(2,1)S(1)}, u32[]{:S(2)}, u32[]{:S(2)}) collective-permute-start(bf16[10,128,128]{1,2,0:T(8,128)(2,1)S(1)} %collective-permute-done.2), channel_id=1, source_target_pairs={{0,4},{4,8},{8,12},{12,16},{16,20},{20,24},{24,28},{28,0},{1,5},{5... | collective-permute-start | bytes 983048 | tf_op jit(solution)/shard_map/ppermute | solution.py:19
  44.9 8.3 collective-permute-start.5
  51.8 7.4 collective-permute-start.6
  59.2 116.0 %copy-start.3 = (bf16[80,128,128]{1,2,0:T(8,128)(2,1)}, bf16[80,128,128]{1,2,0:T(8,128)(2,1)S(1)}, u32[]{:S(2)}) copy-start(bf16[80,128,128]{1,2,0:T(8,128)(2,1)S(1)} %constant_dynamic-update-slice_fusion) | copy-start | bytes 7864324
  600.2 188.9 %reduce-scatter.3.cloned.1.call-start = ((), (), s32[]{:S(2)}) async-start(), calls=%async_computation.3 | async-start | bytes 10485760 | tf_op jit(solution)/shard_map/reduce_scatter | solution.py:140
  610.6 5.8 slice-start
  613.5 2.8 slice-start.1
  613.5 3.5 copy-start.1
  619.5 2.7 copy-start
  631.7 5.9 slice-start
  634.7 3.0 slice-start.1
  634.7 3.7 copy-start.1
  640.9 2.7 copy-start
  653.0 5.8 slice-start
  656.0 2.8 slice-start.1
  656.0 3.5 copy-start.1
  662.0 2.7 copy-start
  674.2 5.8 slice-start
  677.2 2.8 slice-start.1
  677.2 3.6 copy-start.1
  683.2 2.7 copy-start
  695.4 5.8 slice-start
  698.4 2.8 slice-start.1
  698.4 3.5 copy-start.1
  704.4 2.7 copy-start
  716.6 5.8 slice-start
  719.5 3.1 slice-start.1
  719.5 3.9 copy-start.1
  725.9 2.7 copy-start
  738.0 5.8 slice-start
  741.0 2.8 slice-start.1
  741.0 3.5 copy-start.1
  747.0 2.7 copy-start
  759.1 5.8 slice-start
  762.1 2.8 slice-start.1
  762.1 3.6 copy-start.1
  776.1 13.0 %copy-start.2 = (bf16[128,8192]{1,0:T(8,128)(2,1)S(1)}, bf16[128,8192]{1,0:T(8,128)(2,1)}, u32[]{:S(2)}) copy-start(bf16[128,8192]{1,0:T(8,128)(2,1)} %param.14) | copy-start | bytes 6291460
  776.1 13.0 %copy-start.5 = (f32[8192]{0:T(1024)S(1)}, f32[8192]{0:T(1024)}, u32[]{:S(2)}) copy-start(f32[8192]{0:T(1024)} %param.15) | copy-start | bytes 98308
  776.1 13.0 %copy-start.7 = (f32[128]{0:T(128)S(1)}, f32[128]{0:T(128)}, u32[]{:S(2)}) copy-start(f32[128]{0:T(128)} %copy-done.6) | copy-start | bytes 1540
  (2 other events, 3.3 us)
Sparse Core Ops, SparseCore 0:
  13.6 152.3 all-gather.2
  600.3 41.8 reduce-scatter.4
  644.6 144.4 reduce-scatter.2
